TPU v7x, 256 devices: a whole 4x4x8 slice. The times are simulated.
256 devices in a mesh: elem: 64 (over z, x, core), band: 4 (over y).
Axes of the slice: x: 4, y: 4, z: 8, core: 2. Of those that a mesh axis runs over, the one named last changes fastest.
Arguments:
- sw_tau: bfloat16 [32, 224, 16384], P(None, 'band', 'elem'), may hold values from 0.0049743652 to 0.3984375
- sw_ssa: bfloat16 [32, 224, 16384], P(None, 'band', 'elem'), may hold values from 0 to 0.94921875
- lw_tau: bfloat16 [32, 224, 16384], P(None, 'band', 'elem'), may hold values from 0.0099487305 to 2
- lw_source: bfloat16 [32, 224, 16384], P(None, 'band', 'elem'), may hold values from 0.29882812 to 3
- cosine: float32 [16384], P('elem'), may hold values from 0.2 to 1
- surface_albedo: float32 [14, 16384], P(None, 'elem'), may hold values from 0.05 to 0.8
- lit_mask: int32 [16384], P('elem'), may hold values from 0 to 1, as said below
- column_map: int32 [16384], P('elem'), may hold values from 0 to 16383, as said below
- band_solar: float32 [14], replicated, may hold values from 4 to 16
- band_table: int32 [224], P('band'), may hold values from 0 to 13
Outputs:
- heating: float32 [2, 32, 16384], P(None, 'band', 'elem')
Inputs may be any that keep to these rules, and one draw needn't show every extreme that they name: `column_map`: A permutation of the columns; the 256 entries of each index of elem name exactly 256 / 64 positions in the block of 256 span positions of every index of elem. `lit_mask`: index i and index i + 64 / 2 of elem (modulo 64) together hold exactly 256 lit columns; in every draw some index of elem has all its columns lit.
All inputs are finite; a program needn't handle non-finite values.
Results may differ from a plain program's by a relative error of at most 0.0035.
Values may be sent and summed in bfloat16 or wider, within the bound.
A program may use at most 128 MiB of HBM per device.

v0:
```python
import functools
import math

import jax
import jax.numpy as jnp
from jax import lax
from jax.experimental import pallas as pl
from jax.experimental.pallas import tpu as pltpu
from jax.sharding import PartitionSpec as P

F = jnp.float32
B = jnp.bfloat16
LOG2E = math.log2(math.e)
DIFFUSE = -1.66 * LOG2E
Z, X, CORES, BANDS = 8, 4, 2, 4
ELEMS = Z * X * CORES
LEVELS, POINTS, COLS, ALBEDOS = 32, 56, 256, 14
SHARE = COLS // ELEMS
OUT_LEVELS = LEVELS // BANDS


def elem_offsets():
    offsets = [(a, b, c) for a in range(Z) for b in range(X) for c in range(CORES)][1:]
    return sorted(offsets, key=lambda o: -(min(o[0], Z - o[0]) + min(o[1], X - o[1])))


def iota(shape, dim):
    return lax.broadcasted_iota(jnp.int32, shape, dim)


def over_points(x):
    return jnp.sum(x.reshape(POINTS // 8, 8, x.shape[-1]), axis=0)


def pieces(x, n):
    out = []
    for _ in range(n):
        part = x.astype(B).astype(F)
        out.append(part)
        x = x - part
    return out


def spread(rows, onehot):
    tiled = jnp.concatenate([rows] * SHARE, axis=0)
    picked = jnp.dot(onehot, tiled.T.astype(B), preferred_element_type=F)
    lane_share = iota((ELEMS, 128), 1) // 32
    out = jnp.zeros((ELEMS, 128), F)
    for s in range(SHARE):
        out = jnp.where(lane_share == s, picked[s * ELEMS : (s + 1) * ELEMS], out)
    return out


def collect(received, onehot):
    turned = received.T.astype(B)
    out = jnp.zeros((32, COLS), F)
    for s in range(SHARE):
        out = out + jnp.dot(
            turned[s * 32 : (s + 1) * 32],
            onehot[s * ELEMS : (s + 1) * ELEMS],
            preferred_element_type=F,
        )
    return out


def kernel(
    sw_tau, sw_ssa, lw_tau, lw_source, cosine_h, albedo_h, lit_h, map_h, solar_h, table_h,
    out,
    cosine, albedo, lit, column_map, solar, table,
    tau_v, ssa_v, ltau_v, lsrc_v, work_a, work_b, sums, onehot_dyn, onehot_span, params,
    ask_out, ask_in, tell_out, tell_in, give_out, give_in,
    lw_out, lw_in, sw_out, sw_in,
    load_sems, send_sems, recv_sems,
):
    me, band = lax.axis_index("elem"), lax.axis_index("band")
    z, x, core = me // (X * CORES), (me // CORES) % X, me % CORES
    elem_peers = [
        (((z + a) % Z) * (X * CORES) + ((x + b) % X) * CORES + (core + c) % CORES)
        for a, b, c in elem_offsets()
    ]
    band_peers = [(band + i) % BANDS for i in (2, 1, 3)]
    mesh_ids = pl.DeviceIdType.MESH

    map_load = pltpu.make_async_copy(map_h, column_map, load_sems.at[0])
    map_load.start()
    barrier = pltpu.get_barrier_semaphore()
    for p in elem_peers:
        pl.semaphore_signal(barrier, inc=1, device_id=(p, band), device_id_type=mesh_ids)
    for p in band_peers:
        pl.semaphore_signal(barrier, inc=1, device_id=(me, p), device_id_type=mesh_ids)

    loads = [
        pltpu.make_async_copy(src, dst, load_sems.at[1 + i])
        for i, (src, dst) in enumerate(
            [
                (lw_tau, ltau_v), (lw_source, lsrc_v), (sw_tau, tau_v), (sw_ssa, ssa_v),
                (cosine_h, cosine), (albedo_h, albedo), (lit_h, lit), (solar_h, solar), (table_h, table),
            ]
        )
    ]
    for copy in loads:
        copy.start()

    def send_rows(src, dst, i):
        for p in elem_peers:
            pltpu.make_async_remote_copy(
                src_ref=src.at[p],
                dst_ref=dst.at[me],
                send_sem=send_sems.at[i],
                recv_sem=recv_sems.at[i],
                device_id=(p, band),
                device_id_type=mesh_ids,
            ).start()
        dst[pl.ds(me, 1)] = src[pl.ds(me, 1)]

    def rows_of(ref):
        return ref.at[pl.ds(0, ELEMS - 1)]

    def wait_rows(ref, i, sems):
        pltpu.make_async_copy(rows_of(ref), rows_of(ref), sems.at[i]).wait()

    def send_levels(src, dst, i):
        for p in band_peers:
            pltpu.make_async_remote_copy(
                src_ref=src.at[p],
                dst_ref=dst.at[band],
                send_sem=send_sems.at[i],
                recv_sem=recv_sems.at[i],
                device_id=(me, p),
                device_id_type=mesh_ids,
            ).start()

    def wait_levels(ref, i, sems):
        part = ref.at[pl.ds(0, BANDS - 1)]
        pltpu.make_async_copy(part, part, sems.at[i]).wait()

    def total_levels(src, dst):
        total = src[band]
        for p in band_peers:
            total = total + dst[p]
        return total

    map_load.wait()
    place = column_map[...]
    owner, slot = place >> 8, place & 255
    turned = jnp.broadcast_to(place.astype(F), (8, COLS)).T[:, 0:1].astype(jnp.int32)
    earlier = ((turned >> 8) == owner) & (iota((COLS, COLS), 0) < iota((COLS, COLS), 1))
    rank = jnp.sum(earlier.astype(F), axis=0, keepdims=True).astype(jnp.int32)
    key = owner + rank * ELEMS
    onehot_dyn[...] = (key == iota((COLS, COLS), 0)).astype(F).astype(B)
    slots = jnp.broadcast_to((turned & 255).astype(F), (COLS, 128)).astype(B)
    asked = jnp.dot(onehot_dyn[...], slots, preferred_element_type=F)
    lane = iota((ELEMS, 128), 1)
    asking = jnp.zeros((ELEMS, 128), F)
    for s in range(SHARE):
        asking = jnp.where(lane == s, asked[s * ELEMS : (s + 1) * ELEMS], asking)
    ask_out[:, 0, :] = asking

    pl.semaphore_wait(barrier, len(elem_peers) + len(band_peers))
    send_rows(ask_out, ask_in, 0)

    for copy in loads[4:]:
        copy.wait()
    high, low = pieces(albedo[...], 2)
    params[...] = jnp.zeros((32, COLS), F)
    params[0:ALBEDOS] = high
    params[16 : 16 + ALBEDOS] = low
    first, second, third = pieces(cosine[...], 3)
    params[14:15] = first
    params[15:16] = second
    params[30:31] = third

    loads[0].wait()
    loads[1].wait()

    def lw_down(k, down):
        planck = lsrc_v[k].astype(F)
        trans = jnp.exp2(ltau_v[k].astype(F) * DIFFUSE)
        emitted = planck - planck * trans
        work_a[k] = trans
        work_b[k] = emitted
        sums[k] = over_points(down)
        return trans * down + emitted

    down = lax.fori_loop(0, LEVELS, lw_down, jnp.zeros((POINTS, COLS), F), unroll=2)
    surface = lsrc_v[LEVELS - 1].astype(F)
    sums[LEVELS] = over_points(down - surface)

    def lw_up(i, up):
        k = LEVELS - 1 - i
        up = work_a[k] * up + work_b[k]
        sums[k] = sums[k] - over_points(up)
        return up

    lax.fori_loop(0, LEVELS, lw_up, surface, unroll=2)

    def layers():
        return jnp.sum(sums[0:LEVELS] - sums[1 : LEVELS + 1], axis=1)

    lw_out[...] = layers().reshape(BANDS, OUT_LEVELS, COLS)
    send_levels(lw_out, lw_in, 3)

    wait_rows(ask_in, 0, recv_sems)
    asked_of_me = ask_in[:, 0, :].astype(jnp.int32)
    position = iota((ELEMS, COLS), 1)
    for s in range(SHARE):
        onehot_span[s * ELEMS : (s + 1) * ELEMS] = (
            (asked_of_me[:, s : s + 1] == position).astype(F).astype(B)
        )
    tell_out[:, 0, :] = spread(params[...], onehot_span[...])
    send_rows(tell_out, tell_in, 1)

    loads[2].wait()
    loads[3].wait()

    def sw_before(i, carry):
        depth, above = carry
        k = LEVELS - 1 - i
        depth = depth + tau_v[i].astype(F) * (1.0 - 0.5 * ssa_v[i].astype(F))
        above = above * jnp.exp2(tau_v[k].astype(F) * DIFFUSE)
        work_a[i] = depth
        work_b[k] = above
        return depth, above

    lax.fori_loop(
        0, LEVELS, sw_before, (jnp.zeros((POINTS, COLS), F), jnp.ones((POINTS, COLS), F)), unroll=2
    )
    diagonal = iota((POINTS, POINTS), 0) == iota((POINTS, POINTS), 1)
    group = jnp.sum(
        jnp.where(diagonal, table[...].astype(F), 0.0), axis=1, keepdims=True
    ).astype(jnp.int32)
    solar_g = jnp.sum(
        jnp.where(iota((POINTS, ALBEDOS), 1) == group, solar[...], 0.0), axis=1, keepdims=True
    )
    lanes = iota((POINTS, 32), 1)
    picks = ((lanes == group) | (lanes == group + 16)).astype(F).astype(B)

    wait_rows(tell_in, 1, recv_sems)
    told = collect(tell_in[:, 0, :], onehot_dyn[...])
    cosine_d = told[14:15] + told[15:16] + told[30:31]
    albedo_g = jnp.dot(picks, told.astype(B), preferred_element_type=F)
    slant = -LOG2E / cosine_d
    top = solar_g * cosine_d
    bottom = top * jnp.exp2(work_a[LEVELS - 1] * slant)
    upward = albedo_g * bottom
    sums[0] = over_points(top - upward * work_b[0])
    sums[LEVELS] = over_points(bottom - upward)

    def sw_net(k, carry):
        sums[k] = over_points(top * jnp.exp2(work_a[k - 1] * slant) - upward * work_b[k])
        return carry

    lax.fori_loop(1, LEVELS, sw_net, 0)
    sw_out[...] = layers().reshape(BANDS, OUT_LEVELS, COLS)
    send_levels(sw_out, sw_in, 4)
    wait_levels(lw_in, 3, recv_sems)
    scale = 1.0 / (POINTS * BANDS)
    out[1] = total_levels(lw_out, lw_in) * scale

    wait_levels(sw_in, 4, recv_sems)
    total = total_levels(sw_out, sw_in) * scale
    parts = pieces(total, 3) + [jnp.zeros_like(total)]
    give_out[:, 0, :] = spread(jnp.concatenate(parts, axis=0), onehot_dyn[...])
    send_rows(give_out, give_in, 2)
    wait_rows(give_in, 2, recv_sems)
    given = collect(give_in[:, 0, :], onehot_span[...])
    heat = given[0:8] + given[8:16] + given[16:24]
    out[0] = heat * lit[...].astype(F)

    for i, ref in enumerate((ask_out, tell_out, give_out)):
        wait_rows(ref, i, send_sems)
    for i, ref in ((3, lw_out), (4, sw_out)):
        wait_levels(ref, i, send_sems)


def local(
    sw_tau, sw_ssa, lw_tau, lw_source, cosine, surface_albedo, lit_mask, column_map, band_solar, band_table
):
    optics = pltpu.VMEM((LEVELS, POINTS, COLS), B)
    work = pltpu.VMEM((LEVELS, POINTS, COLS), F)
    rows = pltpu.VMEM((ELEMS, 1, 128), F)
    levels = pltpu.VMEM((BANDS, OUT_LEVELS, COLS), F)
    in_hbm = pl.BlockSpec(memory_space=pltpu.HBM)
    in_vmem = pl.BlockSpec(memory_space=pltpu.VMEM)
    return pl.pallas_call(
        kernel,
        out_shape=jax.ShapeDtypeStruct((2, OUT_LEVELS, COLS), F),
        in_specs=[in_hbm] * 10,
        out_specs=in_vmem,
        scratch_shapes=[
            pltpu.VMEM((1, COLS), F),
            pltpu.VMEM((ALBEDOS, COLS), F),
            pltpu.VMEM((1, COLS), jnp.int32),
            pltpu.VMEM((1, COLS), jnp.int32),
            pltpu.VMEM((1, ALBEDOS), F),
            pltpu.VMEM((1, POINTS), jnp.int32),
            optics, optics, optics, optics, work, work,
            pltpu.VMEM((LEVELS + 1, 8, COLS), F),
            pltpu.VMEM((COLS, COLS), B),
            pltpu.VMEM((COLS, COLS), B),
            pltpu.VMEM((32, COLS), F),
            rows, rows, rows, rows, rows, rows,
            levels, levels, levels, levels,
            pltpu.SemaphoreType.DMA((10,)),
            pltpu.SemaphoreType.DMA((5,)),
            pltpu.SemaphoreType.DMA((5,)),
        ],
        compiler_params=pltpu.CompilerParams(
            collective_id=0, has_side_effects=True, vmem_limit_bytes=(64 * 1024 - 512) * 1024
        ),
    )(
        sw_tau, sw_ssa, lw_tau, lw_source,
        cosine.reshape(1, COLS), surface_albedo, lit_mask.reshape(1, COLS),
        column_map.reshape(1, COLS), band_solar.reshape(1, ALBEDOS), band_table.reshape(1, POINTS),
    )


def solution(mesh):
    placed = (
        P(None, "band", "elem"),
        P(None, "band", "elem"),
        P(None, "band", "elem"),
        P(None, "band", "elem"),
        P("elem"),
        P(None, "elem"),
        P("elem"),
        P("elem"),
        P(),
        P("band"),
    )
    return jax.shard_map(
        local, mesh=mesh, in_specs=placed, out_specs=P(None, "band", "elem"), check_vma=False
    )
```

profile of v0, /device:TPU:1, one launch (start us, length us, event | category | flops | bytes accessed | tf_op | source)
XLA Modules:
  0.0 35.2 jit_solution(4084790001945300661)
XLA Ops:
  0.0 33.9 %shard_map.100 = f32[2,8,256]{2,1,0:T(8,128)} custom-call(bf16[32,56,256]{2,1,0:T(8,128)(2,1)} %sw_tau.1, bf16[32,56,256]{2,1,0:T(8,128)(2,1)} %sw_ssa.1, bf16[32,56,256]{2,1,0:T(8,128)(2,1)} %lw_tau.1, bf16[32,56,256]{2,1,0:T(8,128)(2,1)} %lw_source.1, f32[1,256]{1,0:T(1,128)} %bitcast.5, f32[14,256]{1,0:T(8,128)} %albedo_h.1, s32[1,256]{1,0:T(1,128)} %bitcast.6, ...), custom_call_target="tpu_custom_call" | custom-call | tf_op jit(solution)/shard_map/pallas_call | solution.py:285
  33.9 1.3 %copy.12 = f32[2,8,256]{2,1,0:T(8,128)} copy(f32[2,8,256]{2,1,0:T(8,128)} %shard_map.100) | data formatting | bytes 32768
where the time goes:
time: 35.4 us; the launch traced here: 35.2 us
  Pallas kernels  33.9 us (96%)
  local copies, waits for them, and re-layouts  1.32 us (4%)
    pallas_call x1, Pallas kernels, local(): pl.pallas_call(kernel, out_shape=jax.ShapeDtypeStruct((2, OUT_LEVELS, COL...  33.9 us
    unnamed x1, local copies, waits for them, and re-layouts  1.32 us

commit v1 on v0

--- a/solution.py
+++ b/solution.py
@@ -284,7 +284,7 @@
     in_vmem = pl.BlockSpec(memory_space=pltpu.VMEM)
     return pl.pallas_call(
         kernel,
-        out_shape=jax.ShapeDtypeStruct((2, OUT_LEVELS, COLS), F),
+        out_shape=pltpu.VMEM((2, OUT_LEVELS, COLS), F),
         in_specs=[in_hbm] * 10,
         out_specs=in_vmem,
         scratch_shapes=[

time: 35.4 us -> 34 us (0.960)
  local copies, waits for them, and re-layouts: 1.32 us -> 0.61 us
  Pallas kernels: 33.9 us -> 33.3 us
    unnamed x1, local copies, waits for them, and re-layouts: 1.32 us -> 0.61 us
    pallas_call x1, Pallas kernels: 33.9 us -> 33.3 us  [local(): pl.pallas_call(kernel, out_shape=pltpu.VMEM((2, OUT_LEVELS, COLS), F), in...]
where the time goes in v1:
time: 34 us; the launch traced here: 33.9 us
  Pallas kernels  33.3 us (98%)
  local copies, waits for them, and re-layouts  0.61 us (2%)
    pallas_call x1, Pallas kernels, local(): pl.pallas_call(kernel, out_shape=pltpu.VMEM((2, OUT_LEVELS, COLS), F), in...  33.3 us

profile of v1, /device:TPU:1, one launch (start us, length us, event | category | flops | bytes accessed | tf_op | source)
XLA Modules:
  0.0 33.9 jit_solution(4246128723268811068)
XLA Ops:
  0.0 33.3 %shard_map.100 = f32[2,8,256]{2,1,0:T(8,128)S(1)} custom-call(bf16[32,56,256]{2,1,0:T(8,128)(2,1)} %sw_tau.1, bf16[32,56,256]{2,1,0:T(8,128)(2,1)} %sw_ssa.1, bf16[32,56,256]{2,1,0:T(8,128)(2,1)} %lw_tau.1, bf16[32,56,256]{2,1,0:T(8,128)(2,1)} %lw_source.1, f32[1,256]{1,0:T(1,128)} %bitcast.5, f32[14,256]{1,0:T(8,128)} %albedo_h.1, s32[1,256]{1,0:T(1,128)} %bitcast.6, ...), custom_call_target="tpu_custom_call" | custom-call | tf_op jit(solution)/shard_map/pallas_call | solution.py:285
  33.3 0.6 %copy.12 = f32[2,8,256]{2,1,0:T(8,128)} copy(f32[2,8,256]{2,1,0:T(8,128)S(1)} %shard_map.100) | data formatting | bytes 32768

commit v2 on v1

--- a/solution.py
+++ b/solution.py
@@ -24,6 +24,15 @@
     return sorted(offsets, key=lambda o: -(min(o[0], Z - o[0]) + min(o[1], X - o[1])))
 
 
+def all_offsets():
+    offsets = [
+        (a, b, c, y) for a in range(Z) for b in range(X) for c in range(CORES) for y in range(BANDS)
+    ][1:]
+    return sorted(
+        offsets, key=lambda o: -(min(o[0], Z - o[0]) + min(o[1], X - o[1]) + min(o[3], BANDS - o[3]))
+    )
+
+
 def iota(shape, dim):
     return lax.broadcasted_iota(jnp.int32, shape, dim)
 
@@ -41,9 +50,11 @@
     return out
 
 
-def spread(rows, onehot):
-    tiled = jnp.concatenate([rows] * SHARE, axis=0)
-    picked = jnp.dot(onehot, tiled.T.astype(B), preferred_element_type=F)
+def spread(parts, onehot):
+    picked = jnp.zeros((COLS, 128), F)
+    for rows in parts:
+        tiled = jnp.concatenate([rows] * SHARE, axis=0)
+        picked = picked + jnp.dot(onehot, tiled.T.astype(B), preferred_element_type=F)
     lane_share = iota((ELEMS, 128), 1) // 32
     out = jnp.zeros((ELEMS, 128), F)
     for s in range(SHARE):
@@ -69,7 +80,7 @@
     cosine, albedo, lit, column_map, solar, table,
     tau_v, ssa_v, ltau_v, lsrc_v, work_a, work_b, sums, onehot_dyn, onehot_span, params,
     ask_out, ask_in, tell_out, tell_in, give_out, give_in,
-    lw_out, lw_in, sw_out, sw_in,
+    lw_out, lw_in, mine,
     load_sems, send_sems, recv_sems,
 ):
     me, band = lax.axis_index("elem"), lax.axis_index("band")
@@ -207,7 +218,7 @@
         onehot_span[s * ELEMS : (s + 1) * ELEMS] = (
             (asked_of_me[:, s : s + 1] == position).astype(F).astype(B)
         )
-    tell_out[:, 0, :] = spread(params[...], onehot_span[...])
+    tell_out[:, 0, :] = spread([params[...]], onehot_span[...])
     send_rows(tell_out, tell_in, 1)
 
     loads[2].wait()
@@ -251,26 +262,40 @@
         return carry
 
     lax.fori_loop(1, LEVELS, sw_net, 0)
-    sw_out[...] = layers().reshape(BANDS, OUT_LEVELS, COLS)
-    send_levels(sw_out, sw_in, 4)
+    give_out[:, 0, :] = spread(pieces(layers(), 2), onehot_dyn[...])
+    for a, b, c, y in all_offsets():
+        to = ((z + a) % Z) * (X * CORES) + ((x + b) % X) * CORES + (core + c) % CORES
+        pltpu.make_async_remote_copy(
+            src_ref=give_out.at[to],
+            dst_ref=give_in.at[band * ELEMS + me],
+            send_sem=send_sems.at[2],
+            recv_sem=recv_sems.at[2],
+            device_id=(to, (band + y) % BANDS),
+            device_id_type=mesh_ids,
+        ).start()
+    give_in[pl.ds(band * ELEMS + me, 1)] = give_out[pl.ds(me, 1)]
     wait_levels(lw_in, 3, recv_sems)
     scale = 1.0 / (POINTS * BANDS)
     out[1] = total_levels(lw_out, lw_in) * scale
 
-    wait_levels(sw_in, 4, recv_sems)
-    total = total_levels(sw_out, sw_in) * scale
-    parts = pieces(total, 3) + [jnp.zeros_like(total)]
-    give_out[:, 0, :] = spread(jnp.concatenate(parts, axis=0), onehot_dyn[...])
-    send_rows(give_out, give_in, 2)
-    wait_rows(give_in, 2, recv_sems)
-    given = collect(give_in[:, 0, :], onehot_span[...])
-    heat = given[0:8] + given[8:16] + given[16:24]
+    all_rows = give_in.at[pl.ds(0, BANDS * ELEMS - 1)]
+    pltpu.make_async_copy(all_rows, all_rows, recv_sems.at[2]).wait()
+    given = give_in[:, 0, :].reshape(BANDS, ELEMS, 128)
+    mine[...] = jnp.sum(given, axis=0).T.reshape(SHARE, BANDS, OUT_LEVELS, ELEMS)
+    heat = jnp.zeros((2 * OUT_LEVELS, COLS), F)
+    for s in range(SHARE):
+        heat = heat + jnp.dot(
+            jnp.concatenate(pieces(mine[s, band], 2), axis=0).astype(B),
+            onehot_span[s * ELEMS : (s + 1) * ELEMS],
+            preferred_element_type=F,
+        )
+    heat = (heat[0:OUT_LEVELS] + heat[OUT_LEVELS:]) * scale
     out[0] = heat * lit[...].astype(F)
 
-    for i, ref in enumerate((ask_out, tell_out, give_out)):
+    for i, ref in enumerate((ask_out, tell_out)):
         wait_rows(ref, i, send_sems)
-    for i, ref in ((3, lw_out), (4, sw_out)):
-        wait_levels(ref, i, send_sems)
+    pltpu.make_async_copy(all_rows, all_rows, send_sems.at[2]).wait()
+    wait_levels(lw_out, 3, send_sems)
 
 
 def local(
@@ -299,11 +324,13 @@
             pltpu.VMEM((COLS, COLS), B),
             pltpu.VMEM((COLS, COLS), B),
             pltpu.VMEM((32, COLS), F),
-            rows, rows, rows, rows, rows, rows,
-            levels, levels, levels, levels,
+            rows, rows, rows, rows, rows,
+            pltpu.VMEM((BANDS * ELEMS, 1, 128), F),
+            levels, levels,
+            pltpu.VMEM((SHARE, BANDS, OUT_LEVELS, ELEMS), F),
             pltpu.SemaphoreType.DMA((10,)),
-            pltpu.SemaphoreType.DMA((5,)),
-            pltpu.SemaphoreType.DMA((5,)),
+            pltpu.SemaphoreType.DMA((4,)),
+            pltpu.SemaphoreType.DMA((4,)),
         ],
         compiler_params=pltpu.CompilerParams(
             collective_id=0, has_side_effects=True, vmem_limit_bytes=(64 * 1024 - 512) * 1024

time: 34 us -> 32.7 us (0.962)
  Pallas kernels: 33.3 us -> 32 us
    pallas_call x1, Pallas kernels: 33.3 us -> 32 us  [local(): pl.pallas_call(kernel, out_shape=pltpu.VMEM((2, OUT_LEVELS, COLS), F), in...]
where the time goes in v2:
time: 32.7 us
  Pallas kernels  32 us (98%)
  local copies, waits for them, and re-layouts  0.61 us (2%)
    pallas_call x1, Pallas kernels, local(): pl.pallas_call(kernel, out_shape=pltpu.VMEM((2, OUT_LEVELS, COLS), F), in...  32 us

profile of v2, /device:TPU:1, one launch (start us, length us, event | category | flops | bytes accessed | tf_op | source)
XLA Modules:
  0.0 32.7 jit_solution(8868699268598970462)
XLA Ops:
  0.0 32.0 %shard_map.100 = f32[2,8,256]{2,1,0:T(8,128)S(1)} custom-call(bf16[32,56,256]{2,1,0:T(8,128)(2,1)} %sw_tau.1, bf16[32,56,256]{2,1,0:T(8,128)(2,1)} %sw_ssa.1, bf16[32,56,256]{2,1,0:T(8,128)(2,1)} %lw_tau.1, bf16[32,56,256]{2,1,0:T(8,128)(2,1)} %lw_source.1, f32[1,256]{1,0:T(1,128)} %bitcast.5, f32[14,256]{1,0:T(8,128)} %albedo_h.1, s32[1,256]{1,0:T(1,128)} %bitcast.6, ...), custom_call_target="tpu_custom_call" | custom-call | tf_op jit(solution)/shard_map/pallas_call | solution.py:310
  32.0 0.6 %copy.12 = f32[2,8,256]{2,1,0:T(8,128)} copy(f32[2,8,256]{2,1,0:T(8,128)S(1)} %shard_map.100) | data formatting | bytes 32768

commit v3 on v2

--- a/solution.py
+++ b/solution.py
@@ -17,11 +17,16 @@
 LEVELS, POINTS, COLS, ALBEDOS = 32, 56, 256, 14
 SHARE = COLS // ELEMS
 OUT_LEVELS = LEVELS // BANDS
+NEAR = 4
 
 
 def elem_offsets():
     offsets = [(a, b, c) for a in range(Z) for b in range(X) for c in range(CORES)][1:]
     return sorted(offsets, key=lambda o: -(min(o[0], Z - o[0]) + min(o[1], X - o[1])))
+
+
+def far_offsets():
+    return [o for o in elem_offsets() if min(o[0], Z - o[0]) + min(o[1], X - o[1]) > NEAR]
 
 
 def all_offsets():
@@ -50,14 +55,19 @@
     return out
 
 
+def tiled(rows):
+    return jnp.concatenate([rows.astype(B)] * SHARE, axis=0)
+
+
 def spread(parts, onehot):
-    picked = jnp.zeros((COLS, 128), F)
-    for rows in parts:
-        tiled = jnp.concatenate([rows] * SHARE, axis=0)
-        picked = picked + jnp.dot(onehot, tiled.T.astype(B), preferred_element_type=F)
+    picked = [
+        lax.dot_general(onehot, rows, (((1,), (1,)), ((), ())), preferred_element_type=F)
+        for rows in parts
+    ]
+    picked = functools.reduce(jnp.add, picked)
     lane_share = iota((ELEMS, 128), 1) // 32
-    out = jnp.zeros((ELEMS, 128), F)
-    for s in range(SHARE):
+    out = picked[:ELEMS]
+    for s in range(1, SHARE):
         out = jnp.where(lane_share == s, picked[s * ELEMS : (s + 1) * ELEMS], out)
     return out
 
@@ -80,15 +90,20 @@
     cosine, albedo, lit, column_map, solar, table,
     tau_v, ssa_v, ltau_v, lsrc_v, work_a, work_b, sums, onehot_dyn, onehot_span, params,
     ask_out, ask_in, tell_out, tell_in, give_out, give_in,
-    lw_out, lw_in, mine,
+    lw_out, lw_in, mine, telling, ask_far, push_out, push_in, slot_of,
     load_sems, send_sems, recv_sems,
 ):
     me, band = lax.axis_index("elem"), lax.axis_index("band")
     z, x, core = me // (X * CORES), (me // CORES) % X, me % CORES
-    elem_peers = [
-        (((z + a) % Z) * (X * CORES) + ((x + b) % X) * CORES + (core + c) % CORES)
-        for a, b, c in elem_offsets()
-    ]
+
+
+    def at(a, b, c):
+        return ((z + a) % Z) * (X * CORES) + ((x + b) % X) * CORES + (core + c) % CORES
+
+    far = far_offsets()
+    far_peers = [at(*o) for o in far]
+    near_peers = [at(*o) for o in elem_offsets() if o not in far]
+    elem_peers = far_peers + near_peers
     band_peers = [(band + i) % BANDS for i in (2, 1, 3)]
     mesh_ids = pl.DeviceIdType.MESH
 
@@ -112,8 +127,8 @@
     for copy in loads:
         copy.start()
 
-    def send_rows(src, dst, i):
-        for p in elem_peers:
+    def send_rows(src, dst, i, peers):
+        for p in peers:
             pltpu.make_async_remote_copy(
                 src_ref=src.at[p],
                 dst_ref=dst.at[me],
@@ -122,13 +137,13 @@
                 device_id=(p, band),
                 device_id_type=mesh_ids,
             ).start()
+
+    def wait_rows(ref, i, sems, peers):
+        rows = ref.at[pl.ds(0, len(peers))]
+        pltpu.make_async_copy(rows, rows, sems.at[i]).wait()
+
+    def own_row(src, dst):
         dst[pl.ds(me, 1)] = src[pl.ds(me, 1)]
-
-    def rows_of(ref):
-        return ref.at[pl.ds(0, ELEMS - 1)]
-
-    def wait_rows(ref, i, sems):
-        pltpu.make_async_copy(rows_of(ref), rows_of(ref), sems.at[i]).wait()
 
     def send_levels(src, dst, i):
         for p in band_peers:
@@ -168,7 +183,7 @@
     ask_out[:, 0, :] = asking
 
     pl.semaphore_wait(barrier, len(elem_peers) + len(band_peers))
-    send_rows(ask_out, ask_in, 0)
+    send_rows(ask_out, ask_in, 0, near_peers)
 
     for copy in loads[4:]:
         copy.wait()
@@ -180,6 +195,21 @@
     params[14:15] = first
     params[15:16] = second
     params[30:31] = third
+    telling[...] = tiled(params[...])
+    push_out[...] = params[0:16].astype(B)
+    slot_of[...] = (slot == iota((COLS, COLS), 0)).astype(F).astype(B)
+
+    for f, (a, b, c) in enumerate(far):
+        pltpu.make_async_remote_copy(
+            src_ref=push_out,
+            dst_ref=push_in.at[far.index(((Z - a) % Z, (X - b) % X, c))],
+            send_sem=send_sems.at[4],
+            recv_sem=recv_sems.at[4],
+            device_id=(far_peers[f], band),
+            device_id_type=mesh_ids,
+        ).start()
+    send_rows(ask_out, ask_far, 5, far_peers)
+    own_row(ask_out, ask_in)
 
     loads[0].wait()
     loads[1].wait()
@@ -211,15 +241,23 @@
     lw_out[...] = layers().reshape(BANDS, OUT_LEVELS, COLS)
     send_levels(lw_out, lw_in, 3)
 
-    wait_rows(ask_in, 0, recv_sems)
-    asked_of_me = ask_in[:, 0, :].astype(jnp.int32)
-    position = iota((ELEMS, COLS), 1)
-    for s in range(SHARE):
-        onehot_span[s * ELEMS : (s + 1) * ELEMS] = (
-            (asked_of_me[:, s : s + 1] == position).astype(F).astype(B)
-        )
-    tell_out[:, 0, :] = spread([params[...]], onehot_span[...])
-    send_rows(tell_out, tell_in, 1)
+    row = iota((ELEMS, 128), 0)
+    apart_z, apart_x = ((row >> 3) - z) & (Z - 1), ((row >> 1) - x) & (X - 1)
+    near = jnp.minimum(apart_z, Z - apart_z) + jnp.minimum(apart_x, X - apart_x) <= NEAR
+
+    def find_span(asked_of_me):
+        asked_of_me = asked_of_me.astype(jnp.int32)
+        position = iota((ELEMS, COLS), 1)
+        for s in range(SHARE):
+            onehot_span[s * ELEMS : (s + 1) * ELEMS] = (
+                (asked_of_me[:, s : s + 1] == position).astype(F).astype(B)
+            )
+
+    wait_rows(ask_in, 0, recv_sems, near_peers)
+    find_span(jnp.where(near, ask_in[:, 0, :], -1.0))
+    tell_out[:, 0, :] = spread([telling[...]], onehot_span[...])
+    send_rows(tell_out, tell_in, 1, near_peers)
+    own_row(tell_out, tell_in)
 
     loads[2].wait()
     loads[3].wait()
@@ -246,8 +284,17 @@
     lanes = iota((POINTS, 32), 1)
     picks = ((lanes == group) | (lanes == group + 16)).astype(F).astype(B)
 
-    wait_rows(tell_in, 1, recv_sems)
-    told = collect(tell_in[:, 0, :], onehot_dyn[...])
+    pltpu.make_async_copy(push_in, push_in, recv_sems.at[4]).wait()
+    pushed = jnp.dot(
+        push_in[...].reshape(len(far) * 16, COLS), slot_of[...], preferred_element_type=F
+    ).reshape(len(far), 16, COLS)
+    from_far = jnp.zeros((16, COLS), F)
+    for f, p in enumerate(far_peers):
+        from_far = jnp.where(owner == p, pushed[f], from_far)
+
+    wait_rows(tell_in, 1, recv_sems, near_peers)
+    told = collect(jnp.where(near, tell_in[:, 0, :], 0.0), onehot_dyn[...])
+    told = jnp.concatenate([told[0:16] + from_far, told[16:32]], axis=0)
     cosine_d = told[14:15] + told[15:16] + told[30:31]
     albedo_g = jnp.dot(picks, told.astype(B), preferred_element_type=F)
     slant = -LOG2E / cosine_d
@@ -261,10 +308,10 @@
         sums[k] = over_points(top * jnp.exp2(work_a[k - 1] * slant) - upward * work_b[k])
         return carry
 
-    lax.fori_loop(1, LEVELS, sw_net, 0)
-    give_out[:, 0, :] = spread(pieces(layers(), 2), onehot_dyn[...])
+    lax.fori_loop(1, LEVELS, sw_net, 0, unroll=31)
+    give_out[:, 0, :] = spread([tiled(p) for p in pieces(layers(), 2)], onehot_dyn[...])
     for a, b, c, y in all_offsets():
-        to = ((z + a) % Z) * (X * CORES) + ((x + b) % X) * CORES + (core + c) % CORES
+        to = at(a, b, c)
         pltpu.make_async_remote_copy(
             src_ref=give_out.at[to],
             dst_ref=give_in.at[band * ELEMS + me],
@@ -278,6 +325,8 @@
     scale = 1.0 / (POINTS * BANDS)
     out[1] = total_levels(lw_out, lw_in) * scale
 
+    wait_rows(ask_far, 5, recv_sems, far_peers)
+    find_span(jnp.where(near, ask_in[:, 0, :], ask_far[:, 0, :]))
     all_rows = give_in.at[pl.ds(0, BANDS * ELEMS - 1)]
     pltpu.make_async_copy(all_rows, all_rows, recv_sems.at[2]).wait()
     given = give_in[:, 0, :].reshape(BANDS, ELEMS, 128)
@@ -292,8 +341,10 @@
     heat = (heat[0:OUT_LEVELS] + heat[OUT_LEVELS:]) * scale
     out[0] = heat * lit[...].astype(F)
 
-    for i, ref in enumerate((ask_out, tell_out)):
-        wait_rows(ref, i, send_sems)
+    wait_rows(ask_out, 0, send_sems, near_peers)
+    wait_rows(tell_out, 1, send_sems, near_peers)
+    wait_rows(ask_out, 5, send_sems, far_peers)
+    pltpu.make_async_copy(push_in, push_in, send_sems.at[4]).wait()
     pltpu.make_async_copy(all_rows, all_rows, send_sems.at[2]).wait()
     wait_levels(lw_out, 3, send_sems)
 
@@ -328,9 +379,14 @@
             pltpu.VMEM((BANDS * ELEMS, 1, 128), F),
             levels, levels,
             pltpu.VMEM((SHARE, BANDS, OUT_LEVELS, ELEMS), F),
+            pltpu.VMEM((SHARE * 32, COLS), B),
+            rows,
+            pltpu.VMEM((16, COLS), B),
+            pltpu.VMEM((len(far_offsets()), 16, COLS), B),
+            pltpu.VMEM((COLS, COLS), B),
             pltpu.SemaphoreType.DMA((10,)),
-            pltpu.SemaphoreType.DMA((4,)),
-            pltpu.SemaphoreType.DMA((4,)),
+            pltpu.SemaphoreType.DMA((6,)),
+            pltpu.SemaphoreType.DMA((6,)),
         ],
         compiler_params=pltpu.CompilerParams(
             collective_id=0, has_side_effects=True, vmem_limit_bytes=(64 * 1024 - 512) * 1024

time: 32.7 us -> 31.4 us (0.960)
  Pallas kernels: 32 us -> 30.7 us
    pallas_call x1, Pallas kernels: 32 us -> 30.7 us  [local(): pl.pallas_call(kernel, out_shape=pltpu.VMEM((2, OUT_LEVELS, COLS), F), in...]
where the time goes in v3:
time: 31.4 us; the launch traced here: 31.3 us
  Pallas kernels  30.7 us (98%)
  local copies, waits for them, and re-layouts  0.61 us (2%)
    pallas_call x1, Pallas kernels, local(): pl.pallas_call(kernel, out_shape=pltpu.VMEM((2, OUT_LEVELS, COLS), F), in...  30.7 us

profile of v3, /device:TPU:1, one launch (start us, length us, event | category | flops | bytes accessed | tf_op | source)
XLA Modules:
  0.0 31.3 jit_solution(10658075063774402391)
XLA Ops:
  0.0 30.7 %shard_map.100 = f32[2,8,256]{2,1,0:T(8,128)S(1)} custom-call(bf16[32,56,256]{2,1,0:T(8,128)(2,1)} %sw_tau.1, bf16[32,56,256]{2,1,0:T(8,128)(2,1)} %sw_ssa.1, bf16[32,56,256]{2,1,0:T(8,128)(2,1)} %lw_tau.1, bf16[32,56,256]{2,1,0:T(8,128)(2,1)} %lw_source.1, f32[1,256]{1,0:T(1,128)} %bitcast.5, f32[14,256]{1,0:T(8,128)} %albedo_h.1, s32[1,256]{1,0:T(1,128)} %bitcast.6, ...), custom_call_target="tpu_custom_call" | custom-call | tf_op jit(solution)/shard_map/pallas_call | solution.py:361
  30.7 0.6 %copy.12 = f32[2,8,256]{2,1,0:T(8,128)} copy(f32[2,8,256]{2,1,0:T(8,128)S(1)} %shard_map.100) | data formatting | bytes 32768

commit v4 on v3

--- a/solution.py
+++ b/solution.py
@@ -17,7 +17,7 @@
 LEVELS, POINTS, COLS, ALBEDOS = 32, 56, 256, 14
 SHARE = COLS // ELEMS
 OUT_LEVELS = LEVELS // BANDS
-NEAR = 4
+NEAR = 3
 
 
 def elem_offsets():
@@ -26,7 +26,9 @@
 
 
 def far_offsets():
-    return [o for o in elem_offsets() if min(o[0], Z - o[0]) + min(o[1], X - o[1]) > NEAR]
+    return [
+        (a, b) for a, b, c in elem_offsets() if c == 0 and min(a, Z - a) + min(b, X - b) > NEAR
+    ]
 
 
 def all_offsets():
@@ -101,9 +103,10 @@
         return ((z + a) % Z) * (X * CORES) + ((x + b) % X) * CORES + (core + c) % CORES
 
     far = far_offsets()
-    far_peers = [at(*o) for o in far]
-    near_peers = [at(*o) for o in elem_offsets() if o not in far]
-    elem_peers = far_peers + near_peers
+    push_peers = [at(a, b, 0) for a, b in far]
+    far_peers = [at(*o) for o in elem_offsets() if o[:2] in far]
+    near_peers = [at(*o) for o in elem_offsets() if o[:2] not in far]
+    elem_peers = push_peers + near_peers
     band_peers = [(band + i) % BANDS for i in (2, 1, 3)]
     mesh_ids = pl.DeviceIdType.MESH
 
@@ -199,16 +202,15 @@
     push_out[...] = params[0:16].astype(B)
     slot_of[...] = (slot == iota((COLS, COLS), 0)).astype(F).astype(B)
 
-    for f, (a, b, c) in enumerate(far):
+    for f, (a, b) in enumerate(far):
         pltpu.make_async_remote_copy(
             src_ref=push_out,
-            dst_ref=push_in.at[far.index(((Z - a) % Z, (X - b) % X, c))],
+            dst_ref=push_in.at[core, far.index(((Z - a) % Z, (X - b) % X))],
             send_sem=send_sems.at[4],
             recv_sem=recv_sems.at[4],
-            device_id=(far_peers[f], band),
+            device_id=(push_peers[f], band),
             device_id_type=mesh_ids,
         ).start()
-    send_rows(ask_out, ask_far, 5, far_peers)
     own_row(ask_out, ask_in)
 
     loads[0].wait()
@@ -258,6 +260,7 @@
     tell_out[:, 0, :] = spread([telling[...]], onehot_span[...])
     send_rows(tell_out, tell_in, 1, near_peers)
     own_row(tell_out, tell_in)
+    send_rows(ask_out, ask_far, 5, far_peers)
 
     loads[2].wait()
     loads[3].wait()
@@ -284,16 +287,29 @@
     lanes = iota((POINTS, 32), 1)
     picks = ((lanes == group) | (lanes == group + 16)).astype(F).astype(B)
 
-    pltpu.make_async_copy(push_in, push_in, recv_sems.at[4]).wait()
-    pushed = jnp.dot(
-        push_in[...].reshape(len(far) * 16, COLS), slot_of[...], preferred_element_type=F
-    ).reshape(len(far), 16, COLS)
-    from_far = jnp.zeros((16, COLS), F)
-    for f, p in enumerate(far_peers):
-        from_far = jnp.where(owner == p, pushed[f], from_far)
-
+    def pick_far(c, found):
+        blocks = push_in[c].reshape(len(far) * 16, COLS)
+        picked = jnp.dot(blocks, slot_of[...], preferred_element_type=F)
+        for f, (a, b) in enumerate(far):
+            holder = at(a, b, 0) - core + c
+            found = jnp.where(owner == holder, picked[f * 16 : (f + 1) * 16], found)
+        return found
+
+    one_core = push_in.at[0]
+    pltpu.make_async_copy(one_core, one_core, recv_sems.at[4]).wait()
+    pltpu.make_async_remote_copy(
+        src_ref=push_in.at[core],
+        dst_ref=push_in.at[core],
+        send_sem=send_sems.at[6],
+        recv_sem=recv_sems.at[6],
+        device_id=(at(0, 0, 1), band),
+        device_id_type=mesh_ids,
+    ).start()
+    from_far = pick_far(core, jnp.zeros((16, COLS), F))
     wait_rows(tell_in, 1, recv_sems, near_peers)
     told = collect(jnp.where(near, tell_in[:, 0, :], 0.0), onehot_dyn[...])
+    pltpu.make_async_copy(one_core, one_core, recv_sems.at[6]).wait()
+    from_far = pick_far(1 - core, from_far)
     told = jnp.concatenate([told[0:16] + from_far, told[16:32]], axis=0)
     cosine_d = told[14:15] + told[15:16] + told[30:31]
     albedo_g = jnp.dot(picks, told.astype(B), preferred_element_type=F)
@@ -344,7 +360,8 @@
     wait_rows(ask_out, 0, send_sems, near_peers)
     wait_rows(tell_out, 1, send_sems, near_peers)
     wait_rows(ask_out, 5, send_sems, far_peers)
-    pltpu.make_async_copy(push_in, push_in, send_sems.at[4]).wait()
+    pltpu.make_async_copy(one_core, one_core, send_sems.at[4]).wait()
+    pltpu.make_async_copy(one_core, one_core, send_sems.at[6]).wait()
     pltpu.make_async_copy(all_rows, all_rows, send_sems.at[2]).wait()
     wait_levels(lw_out, 3, send_sems)
 
@@ -382,11 +399,11 @@
             pltpu.VMEM((SHARE * 32, COLS), B),
             rows,
             pltpu.VMEM((16, COLS), B),
-            pltpu.VMEM((len(far_offsets()), 16, COLS), B),
+            pltpu.VMEM((CORES, len(far_offsets()), 16, COLS), B),
             pltpu.VMEM((COLS, COLS), B),
             pltpu.SemaphoreType.DMA((10,)),
-            pltpu.SemaphoreType.DMA((6,)),
-            pltpu.SemaphoreType.DMA((6,)),
+            pltpu.SemaphoreType.DMA((7,)),
+            pltpu.SemaphoreType.DMA((7,)),
         ],
         compiler_params=pltpu.CompilerParams(
             collective_id=0, has_side_effects=True, vmem_limit_bytes=(64 * 1024 - 512) * 1024

time: 31.4 us -> 30.6 us (0.975)
  Pallas kernels: 30.7 us -> 29.9 us
    pallas_call x1, Pallas kernels: 30.7 us -> 29.9 us  [local(): pl.pallas_call(kernel, out_shape=pltpu.VMEM((2, OUT_LEVELS, COLS), F), in...]
where the time goes in v4:
time: 30.6 us; the launch traced here: 30.5 us
  Pallas kernels  29.9 us (98%)
  local copies, waits for them, and re-layouts  0.61 us (2%)
    pallas_call x1, Pallas kernels, local(): pl.pallas_call(kernel, out_shape=pltpu.VMEM((2, OUT_LEVELS, COLS), F), in...  29.9 us

profile of v4, /device:TPU:1, one launch (start us, length us, event | category | flops | bytes accessed | tf_op | source)
XLA Modules:
  0.0 30.5 jit_solution(3965537283281594388)
XLA Ops:
  0.0 29.9 %shard_map.100 = f32[2,8,256]{2,1,0:T(8,128)S(1)} custom-call(bf16[32,56,256]{2,1,0:T(8,128)(2,1)} %sw_tau.1, bf16[32,56,256]{2,1,0:T(8,128)(2,1)} %sw_ssa.1, bf16[32,56,256]{2,1,0:T(8,128)(2,1)} %lw_tau.1, bf16[32,56,256]{2,1,0:T(8,128)(2,1)} %lw_source.1, f32[1,256]{1,0:T(1,128)} %bitcast.5, f32[14,256]{1,0:T(8,128)} %albedo_h.1, s32[1,256]{1,0:T(1,128)} %bitcast.6, ...), custom_call_target="tpu_custom_call" | custom-call | tf_op jit(solution)/shard_map/pallas_call | solution.py:378
  29.9 0.6 %copy.12 = f32[2,8,256]{2,1,0:T(8,128)} copy(f32[2,8,256]{2,1,0:T(8,128)S(1)} %shard_map.100) | data formatting | bytes 32768

commit v5 on v4

--- a/solution.py
+++ b/solution.py
@@ -306,10 +306,10 @@
         device_id_type=mesh_ids,
     ).start()
     from_far = pick_far(core, jnp.zeros((16, COLS), F))
+    pltpu.make_async_copy(one_core, one_core, recv_sems.at[6]).wait()
+    from_far = pick_far(1 - core, from_far)
     wait_rows(tell_in, 1, recv_sems, near_peers)
     told = collect(jnp.where(near, tell_in[:, 0, :], 0.0), onehot_dyn[...])
-    pltpu.make_async_copy(one_core, one_core, recv_sems.at[6]).wait()
-    from_far = pick_far(1 - core, from_far)
     told = jnp.concatenate([told[0:16] + from_far, told[16:32]], axis=0)
     cosine_d = told[14:15] + told[15:16] + told[30:31]
     albedo_g = jnp.dot(picks, told.astype(B), preferred_element_type=F)

time: 30.6 us -> 30.4 us (level)
  no operation moved by 1% of the time
where the time goes in v5:
time: 30.4 us; the launch traced here: 30.3 us
  Pallas kernels  29.7 us (98%)
  local copies, waits for them, and re-layouts  0.61 us (2%)
    pallas_call x1, Pallas kernels, local(): pl.pallas_call(kernel, out_shape=pltpu.VMEM((2, OUT_LEVELS, COLS), F), in...  29.7 us

profile of v5, /device:TPU:1, one launch (start us, length us, event | category | flops | bytes accessed | tf_op | source)
XLA Modules:
  0.0 30.3 jit_solution(17606039626112910023)
XLA Ops:
  0.0 29.7 %shard_map.100 = f32[2,8,256]{2,1,0:T(8,128)S(1)} custom-call(bf16[32,56,256]{2,1,0:T(8,128)(2,1)} %sw_tau.1, bf16[32,56,256]{2,1,0:T(8,128)(2,1)} %sw_ssa.1, bf16[32,56,256]{2,1,0:T(8,128)(2,1)} %lw_tau.1, bf16[32,56,256]{2,1,0:T(8,128)(2,1)} %lw_source.1, f32[1,256]{1,0:T(1,128)} %bitcast.5, f32[14,256]{1,0:T(8,128)} %albedo_h.1, s32[1,256]{1,0:T(1,128)} %bitcast.6, ...), custom_call_target="tpu_custom_call" | custom-call | tf_op jit(solution)/shard_map/pallas_call | solution.py:378
  29.7 0.6 %copy.12 = f32[2,8,256]{2,1,0:T(8,128)} copy(f32[2,8,256]{2,1,0:T(8,128)S(1)} %shard_map.100) | data formatting | bytes 32768

commit v6 on v5

--- a/solution.py
+++ b/solution.py
@@ -317,15 +317,14 @@
     top = solar_g * cosine_d
     bottom = top * jnp.exp2(work_a[LEVELS - 1] * slant)
     upward = albedo_g * bottom
-    sums[0] = over_points(top - upward * work_b[0])
-    sums[LEVELS] = over_points(bottom - upward)
-
-    def sw_net(k, carry):
-        sums[k] = over_points(top * jnp.exp2(work_a[k - 1] * slant) - upward * work_b[k])
-        return carry
-
-    lax.fori_loop(1, LEVELS, sw_net, 0, unroll=31)
-    give_out[:, 0, :] = spread([tiled(p) for p in pieces(layers(), 2)], onehot_dyn[...])
+    below = over_points(bottom - upward)
+    heats = [None] * LEVELS
+    for k in range(LEVELS - 1, -1, -1):
+        direct = top * jnp.exp2(work_a[k - 1] * slant) if k else top
+        here = over_points(direct - upward * work_b[k])
+        heats[k] = jnp.sum(here - below, axis=0, keepdims=True)
+        below = here
+    give_out[:, 0, :] = spread([tiled(p) for p in pieces(jnp.concatenate(heats, axis=0), 2)], onehot_dyn[...])
     for a, b, c, y in all_offsets():
         to = at(a, b, c)
         pltpu.make_async_remote_copy(

time: 30.4 us -> 30.3 us (level)
  no operation moved by 1% of the time
where the time goes in v6:
time: 30.3 us; the launch traced here: 30.2 us
  Pallas kernels  29.6 us (98%)
  local copies, waits for them, and re-layouts  0.61 us (2%)
    pallas_call x1, Pallas kernels, local(): pl.pallas_call(kernel, out_shape=pltpu.VMEM((2, OUT_LEVELS, COLS), F), in...  29.6 us
    unnamed x1, local copies, waits for them, and re-layouts  0.61 us

profile of v6, /device:TPU:1, one launch (start us, length us, event | category | flops | bytes accessed | tf_op | source)
XLA Modules:
  0.0 30.2 jit_solution(10276780704178221049)
XLA Ops:
  0.0 29.6 %shard_map.100 = f32[2,8,256]{2,1,0:T(8,128)S(1)} custom-call(bf16[32,56,256]{2,1,0:T(8,128)(2,1)} %sw_tau.1, bf16[32,56,256]{2,1,0:T(8,128)(2,1)} %sw_ssa.1, bf16[32,56,256]{2,1,0:T(8,128)(2,1)} %lw_tau.1, bf16[32,56,256]{2,1,0:T(8,128)(2,1)} %lw_source.1, f32[1,256]{1,0:T(1,128)} %bitcast.5, f32[14,256]{1,0:T(8,128)} %albedo_h.1, s32[1,256]{1,0:T(1,128)} %bitcast.6, ...), custom_call_target="tpu_custom_call" | custom-call | tf_op jit(solution)/shard_map/pallas_call | solution.py:377
  29.6 0.6 %copy.12 = f32[2,8,256]{2,1,0:T(8,128)} copy(f32[2,8,256]{2,1,0:T(8,128)S(1)} %shard_map.100) | data formatting | bytes 32768
